TPU v7x, 256 devices: a whole 4x4x8 slice. The times are simulated.
256 devices in a mesh: ctx: 32 (over z, x), tp: 8 (over y, core).
Axes of the slice: x: 4, y: 4, z: 8, core: 2. Of those that a mesh axis runs over, the one named last changes fastest.
Arguments:
- lengths: int32 [32], replicated, may hold values from 1 to 288, 6144 in all
- queries: bfloat16 [9216, 8192], P('ctx', 'tp'), may hold values from -10 to 10
- keys: bfloat16 [9216, 1024], P('ctx', 'tp'), may hold values from -6 to 6
- values: bfloat16 [9216, 1024], P('ctx', 'tp'), may hold values from -8 to 8
- out_weight: bfloat16 [8192, 8192], P('tp', 'ctx'), may hold values from -0.125 to 0.125
Outputs:
- mixed: bfloat16 [9216, 8192], P('ctx', 'tp')
All inputs are finite; a program needn't handle non-finite values.
Results may differ from a plain program's by a relative error of at most 0.019.
Values may be sent and summed in bfloat16 or wider, within the bound.
A program may use at most 64 MiB of HBM per device.

v0:
```python
import math

import jax
import jax.numpy as jnp
from jax import lax
from jax.sharding import PartitionSpec as P

HD = 128


def shards(lengths, queries, keys, values, out_weight):
    n_ctx = lax.axis_size("ctx")
    rank_self = lax.axis_index("ctx")
    slots = queries.shape[0]
    head_size = HD
    kv_local = keys.shape[1] // head_size
    group = queries.shape[1] // keys.shape[1]
    scale = head_size ** (-0.5)
    starts = jnp.cumsum(lengths) - lengths
    ranks = jnp.arange(n_ctx, dtype=jnp.int32)

    def lookup(table, device):
        return jnp.sum(jnp.where(ranks == device, table, 0))

    own_length = lookup(lengths, rank_self)
    own_start = lookup(starts, rank_self)
    slot_rows = jnp.arange(slots, dtype=jnp.int32)
    query_pos = own_start + slot_rows
    query_live = slot_rows < own_length
    quad = queries.reshape(slots, kv_local, group, head_size)
    initial = (
        jnp.full((slots, kv_local, group), -1e30, jnp.float32),
        jnp.zeros((slots, kv_local, group), jnp.float32),
        jnp.zeros((slots, kv_local, group, head_size), jnp.float32),
    )
    carry = initial
    key_piece = lax.all_gather(keys, "ctx", axis=0, tiled=True)
    total_rows = key_piece.shape[0]
    width = math.gcd(total_rows, slots)
    count = total_rows // width
    key_blocks = key_piece.reshape(count, width, kv_local, head_size)
    value_blocks = lax.all_gather(values, "ctx", axis=0, tiled=True).reshape(
        count, width, kv_local, head_size
    )

    def compute(state, key_blk, value_blk, begin, device):
        peak, norm, accum = state
        rows_in = jnp.mod(begin, slots) + jnp.arange(width, dtype=jnp.int32)
        key_pos = lookup(starts, device) + rows_in
        allowed = (rows_in < lookup(lengths, device))[None, :] & (
            key_pos[None, :] <= query_pos[:, None]
        )
        allowed = allowed[:, None, None, :]
        scores = (
            jnp.einsum("rkgd,skd->rkgs", quad, key_blk, preferred_element_type=jnp.float32) * scale
        )
        new_peak = jnp.maximum(peak, jnp.max(jnp.where(allowed, scores, -1e30), axis=-1))
        weights = jnp.where(allowed, jnp.exp(scores - new_peak[..., None]), 0.0)
        factor = jnp.exp(peak - new_peak)
        norm = norm * factor + jnp.sum(weights, axis=-1)
        accum = accum * factor[..., None] + jnp.einsum(
            "rkgs,skd->rkgd",
            weights.astype(jnp.bfloat16),
            value_blk,
            preferred_element_type=jnp.float32,
        )
        return (new_peak, norm, accum)

    def step(state, inputs):
        key_blk, value_blk, index = inputs
        begin = index * width
        device = jnp.floor_divide(begin, slots)
        state = lax.cond(
            (device >= 0) & (device <= rank_self),
            lambda s: compute(s, key_blk, value_blk, begin, device),
            lambda s: s,
            state,
        )
        return (state, None)

    carry, _ = lax.scan(step, carry, (key_blocks, value_blocks, jnp.arange(count, dtype=jnp.int32)))
    state = carry
    peak, norm, accum = state
    attn = (accum / norm[..., None]).reshape(slots, kv_local * group * head_size)
    attn = jnp.where(query_live[:, None], attn, 0.0).astype(jnp.bfloat16)
    full_weight = lax.all_gather(out_weight, "ctx", axis=1, tiled=True)
    columns = full_weight.shape[1] // lax.axis_size("tp")
    shaped = full_weight.reshape(full_weight.shape[0], lax.axis_size("tp") * 1, columns)
    mixed = lax.psum_scatter(
        jnp.einsum("rh,hcd->crd", attn, shaped, preferred_element_type=jnp.float32).astype(
            jnp.bfloat16
        ),
        "tp",
        scatter_dimension=0,
        tiled=True,
    ).astype(jnp.float32)
    return mixed[0].astype(jnp.bfloat16)


def solution(mesh):
    return jax.shard_map(
        shards,
        mesh=mesh,
        in_specs=(P(), P("ctx", "tp"), P("ctx", "tp"), P("ctx", "tp"), P("tp", "ctx")),
        out_specs=P("ctx", "tp"),
        check_vma=False,
    )
```

profile of v0, /device:TPU:1, one launch (start us, length us, event | category | flops | bytes accessed | tf_op | source)
XLA Modules:
  0.0 505.4 jit_solution(1490856292367444784)
XLA Ops:
  6.5 0.7 all-gather.4.cloned.1.call-update
  7.3 0.7 all-gather.6.cloned.1.call-update
  8.1 2.0 copy.12
  10.2 0.7 copy.9
  11.1 1.2 copy.16
  12.4 0.6 fusion.36
  13.6 75.0 %all-gather.4.cloned.1.call-done = bf16[9216,128]{1,0:T(8,128)(2,1)} async-done(((bf16[288,128]{1,0:T(8,128)(2,1)}), bf16[9216,128]{1,0:T(8,128)(2,1)}) %all-gather.4.cloned.1.call-update) | async-done | bytes 2359312 | tf_op jit(solution)/shard_map/all_gather | solution.py:37
  88.6 78.2 %all-gather.6.cloned.1.call-done = bf16[9216,128]{1,0:T(8,128)(2,1)} async-done(((bf16[288,128]{1,0:T(8,128)(2,1)}), bf16[9216,128]{1,0:T(8,128)(2,1)}) %all-gather.6.cloned.1.call-update) | async-done | bytes 2359312 | tf_op jit(solution)/shard_map/all_gather | solution.py:42
  166.9 50.1 %while.19 = (s32[]{:T(128)}, f32[288,1,8]{0,2,1:T(8,128)S(1)}, f32[288,1,8]{0,2,1:T(8,128)S(1)}, f32[288,1,8,128]{3,0,2,1:T(8,128)S(1)}, s32[32]{0:T(128)S(1)}, ...) while((s32[]{:T(128)}, f32[288,1,8]{0,2,1:T(8,128)S(1)}, ...), condition=%wide.region_10.11_spmd.clone.clone, body=%wide.region_3.10_spmd.clone.clone.sunk | while | flops 347801920 | bytes 11547871 | solution.py:81
  166.9 0.6 dynamic_slice.42
  168.2 7.5 %conditional.4 = ((f32[288,1,8]{0,2,1:T(8,128)S(1)}, f32[288,1,8]{0,2,1:T(8,128)S(1)}, f32[288,1,8,128]{3,0,2,1:T(8,128)S(1)})) conditional(s32[]{:T(128)} %convert_element_type.47, (f32[288,1,8]{0,2,1:T(8,128)S(1)}, f32[288,1,8]{0,2,1:T(8,128)S(1)}, f32[288,1,8,128]{3,0,2,1:T(8,128)S(1)}) %tuple.61, (s32[]{:T(128)}, s32[]{:T(128)}, s32[32]{0:T(128)S(1)}, ...), branch_computations={%region_4.4_spmd, %region_5.9_spmd} | conditional | flops 347801920 | bytes 11546298 | solution.py:73
  168.2 0.7 fusion.29
  168.9 1.2 fusion.27
  170.1 0.6 fusion.28
  170.9 1.6 fusion.2
  172.6 2.3 fusion.17
  174.9 0.8 fusion.6
  175.7 0.6 dynamic_slice.42
  177.1 0.6 dynamic_slice.42
  178.4 0.6 dynamic_slice.42
  179.7 0.6 dynamic_slice.42
  181.1 0.6 dynamic_slice.42
  182.4 0.6 dynamic_slice.42
  183.7 0.6 dynamic_slice.42
  185.1 0.6 dynamic_slice.42
  186.4 0.6 dynamic_slice.42
  187.7 0.6 dynamic_slice.42
  189.1 0.6 dynamic_slice.42
  190.4 0.6 dynamic_slice.42
  217.9 92.5 %all-gather.8.cloned.1.call-done = bf16[1024,8192]{0,1:T(8,128)(2,1)} async-done(((bf16[1024,256]{0,1:T(8,128)(2,1)}), bf16[1024,8192]{0,1:T(8,128)(2,1)}) %all-gather.8.cloned.1.call-update) | async-done | bytes 16777232 | tf_op jit(solution)/shard_map/all_gather | solution.py:86
  310.4 10.2 %convert_bitcast_fusion = bf16[8,288,1024]{2,1,0:T(8,128)(2,1)} fusion(bf16[288,1024,1]{1,0,2:T(8,128)(2,1)S(1)} %reshape.160, bf16[1024,8,1024]{0,2,1:T(8,128)(2,1)} %bitcast.89), kind=kOutput, calls=%fused_computation.39 | convolution fusion | flops 4834197504 | bytes 22085632 | tf_op jit(solution)/shard_map/rh,hcd->crd/dot_general | solution.py:90
  320.6 178.3 %reduce-scatter.2.cloned.1.call-done = bf16[1,288,1024]{2,1,0:T(8,128)(2,1)} async-done(((bf16[8,288,1024]{2,1,0:T(8,128)(2,1)}), bf16[1,288,1024]{2,1,0:T(8,128)(2,1)}) %reduce-scatter.2.cloned.1.call-update) | async-done | bytes 589840 | tf_op jit(solution)/shard_map/reduce_scatter | solution.py:89
  (105 shorter events, 14.2 us)
Async XLA Ops:
  6.5 5.8 %copy-start = (s32[32]{0:T(128)S(1)}, s32[32]{0:T(128)}, u32[]{:S(2)}) copy-start(s32[32]{0:T(128)} %param.9) | copy-start | bytes 388
  6.5 82.0 %all-gather.4.cloned.1.call-start = ((), (), s32[]{:S(2)}) async-start(), calls=%async_computation.1 | async-start | bytes 2433024 | tf_op jit(solution)/shard_map/all_gather | solution.py:37
  7.3 159.5 %all-gather.6.cloned.1.call-start = ((), (), s32[]{:S(2)}) async-start(), calls=%async_computation.2 | async-start | bytes 2433024 | tf_op jit(solution)/shard_map/all_gather | solution.py:42
  8.0 302.4 %all-gather.8.cloned.1.call-start = ((), (), s32[]{:S(2)}) async-start(), calls=%async_computation.3 | async-start | bytes 17301504 | tf_op jit(solution)/shard_map/all_gather | solution.py:86
  10.1 488.8 %reduce-scatter.2.cloned.1.call-start = ((), (), s32[]{:S(2)}) async-start(), calls=%async_computation.4 | async-start | bytes 5308416 | tf_op jit(solution)/shard_map/reduce_scatter | solution.py:89
Sparse Core Ops, SparseCore 0:
  9.9 78.5 all-gather.3
  91.2 75.5 all-gather.5
  169.4 140.9 all-gather.7
  320.7 178.1 reduce-scatter.1
where the time goes:
time: 511 us; the launch traced here: 505 us
  waiting for transfers between devices  425 us (83%)
  local copies, waits for them, and re-layouts  24.2 us (5%)
  loops' own time  23.1 us (5%)
  matrix products  14.1 us (3%)
  between operations  13.2 us (3%)
  other arithmetic  5.24 us (1%)
    reduce_scatter x1, waiting for transfers between devices, shards(): lax.psum_scatter(jnp.einsum('rh,hcd->crd', attn, shaped, preferred_elemen...  178 us
    all_gather x1, waiting for transfers between devices, shards(): full_weight = lax.all_gather(out_weight, 'ctx', axis=1, tiled=True)  92.5 us
    all_gather x1, waiting for transfers between devices, shards(): lax.all_gather(values, 'ctx', axis=0, tiled=True)  78.2 us
    all_gather x1, waiting for transfers between devices, shards(): key_piece = lax.all_gather(keys, 'ctx', axis=0, tiled=True)  75 us
    another operation x1, loops' own time, shards(): lax.scan(step, carry, (key_blocks, value_blocks, jnp.arange(count, dtype=...  22.6 us
    dynamic_slice x32, local copies, waits for them, and re-layouts, shards(): lax.scan(step, carry, (key_blocks, value_blocks, jnp.arange(count, dtype=...  19.5 us
  transfers between devices with their start and end apart: 4, of which 4 were waited for; matrix products, arithmetic and copies ran while one was open for 7% of the time, Pallas kernels for 0%

commit v1 on v0

v1 whole, which is shorter than its diff:
```python
import math

import jax
import jax.numpy as jnp
from jax import lax
from jax.experimental import pallas as pl
from jax.experimental.pallas import tpu as pltpu
from jax.sharding import PartitionSpec as P

HD = 128
NZ, NX, NY = 8, 4, 4
SLOTS = 288
HEADS = 8
KEYS = NX * SLOTS
HALF = SLOTS // 2
WIDE = 256
DEPTH = 1024
PIECE = DEPTH // 2
UNITS = 2 * NX
SCALE = math.log2(math.e) * HD**-0.5
MESH = pl.DeviceIdType.MESH


def ring(value, size):
    return lax.rem(value + size, size)


def chunk_offset(s):
    odd = lax.rem(s, 2)
    return lax.div(s, 2) * (1 - odd) - lax.div(s + 1, 2) * odd


def unit_place(u):
    g = lax.div(u + 2, 4)
    mid = lax.rem(g, 2)
    i = mid * (1 + lax.rem(u, 2)) + lax.div(g, 2) * 3
    r = mid * lax.div(u + 2 - 4 * mid, 2) + (1 - mid) * lax.rem(u, 2)
    return i, r


def x_offset(i):
    return i + lax.div(i, 2) - 2 * lax.div(i, 3)


def kernel(
    lengths, q, k, v, w, out,
    kv, live, acc, peak, wbuf, abuf, csend, crecv, own, rsend, rrecv, msend, mrecv, fbuf, obuf,
    local, zs, zr, xs1, xr1, xs2, xr2, ws, wr, as1, as2, ar, cs, cr, rs, rr, ms, mr, fs, fr,
):
    me_c = lax.axis_index("ctx")
    me_t = lax.axis_index("tp")
    z, x = lax.div(me_c, NX), lax.rem(me_c, NX)
    y, core = lax.div(me_t, 2), lax.rem(me_t, 2)

    def on_z(d):
        return (ring(z + d, NZ) * NX + x, me_t)

    def on_x(d):
        return (z * NX + ring(x + d, NX), me_t)

    def on_y(d):
        return (me_c, ring(y + d, NY) * 2 + core)

    z_up, z_down = on_z(1), on_z(-1)
    x_right, x_left = on_x(1), on_x(-1)
    y_up, y_down = on_y(1), on_y(-1)
    twin = (me_c, y * 2 + 1 - core)

    def remote(src, dst, send, recv, device):
        return pltpu.make_async_remote_copy(
            src_ref=src, dst_ref=dst, send_sem=send, recv_sem=recv,
            device_id=device, device_id_type=MESH,
        )

    barrier = pltpu.get_barrier_semaphore()
    for device in (z_up, z_down, x_right, x_left, on_x(2), y_up, y_down, twin):
        pl.semaphore_signal(barrier, inc=1, device_id=device, device_id_type=MESH)

    w_copy = pltpu.make_async_copy(w, wbuf.at[z], local.at[0])
    w_copy.start()

    def span(column):
        return pl.ds(pl.multiple_of(column * SLOTS, SLOTS), SLOTS)

    own_length = lengths[me_c]
    mine = span(x)
    alive = lax.broadcasted_iota(jnp.int32, (SLOTS, HD), 0) < own_length
    key = k[...].astype(jnp.float32)
    kv[z, 0, mine, :] = jnp.where(alive, key, key[0:1, :]).astype(jnp.bfloat16)
    kv[z, 1, mine, :] = jnp.where(alive, v[...].astype(jnp.float32), 0.0).astype(jnp.bfloat16)

    pl.semaphore_wait(barrier, 8)

    def z_block(zp):
        return kv.at[zp, :, mine, :]

    def z_both(zp, send, arrival, device):
        return remote(z_block(zp), z_block(zp), zs.at[send], zr.at[arrival], device)

    def z_one(zp, which, send, arrival, device):
        block = kv.at[zp, which, mine, :]
        return remote(block, block, zs.at[send], zr.at[arrival], device)

    def zp_of(s):
        return ring(z + chunk_offset(s), NZ)

    def z_forward(j, act):
        zp = zp_of(j)
        step = 2 * lax.rem(j, 2) - 1
        device = (ring(z + step, NZ) * NX + x, me_t)

        @pl.when(j <= 4)
        def _():
            act(z_both(zp, j, j + 2, device))

        @pl.when(j == 5)
        def _():
            act(z_one(zp, 0, j, 7, device))

        @pl.when(j == 6)
        def _():
            act(z_one(zp, 1, j, 8, device))

    def z_arrival(j):
        zp = zp_of(j)

        @pl.when(j <= 6)
        def _():
            z_both(zp, j, j, z_up).wait_recv()

        @pl.when(j == 7)
        def _():
            z_one(zp, 0, 0, 7, z_up).wait_recv()
            z_one(zp, 1, 0, 8, z_down).wait_recv()

    def x_first(j, way, column):
        zp = zp_of(j)
        block = kv.at[zp, :, span(column), :]
        return remote(block, block, xs1.at[way, j], xr1.at[way, j], (x_right, x_left)[way])

    def x_second(j, way, column):
        zp = zp_of(j)
        block = kv.at[zp, way, span(column), :]
        return remote(block, block, xs2.at[way, j], xr2.at[way, j], (x_right, x_left)[way])

    left, right, across = ring(x - 1, NX), ring(x + 1, NX), ring(x + 2, NX)

    def needed(j):
        return zp_of(j) <= z

    def x_start(j):
        @pl.when(needed(j))
        def _():
            x_first(j, 0, x).start()
            x_first(j, 1, x).start()

    def x_forward(j):
        @pl.when(needed(j))
        def _():
            x_first(j, 0, left).wait_recv()
            x_second(j, 0, left).start()
            x_first(j, 1, right).wait_recv()
            x_second(j, 1, right).start()

    def w_copy_of(i, way, held):
        hop = lax.div(i, 2) + held
        half = lax.rem(i, 2) if way == 0 else 1 - lax.rem(i, 2)
        block = ring(z - hop, NZ) if way == 0 else ring(z + hop, NZ)
        part = wbuf.at[block, pl.ds(pl.multiple_of(half * PIECE, PIECE), PIECE), :]
        return remote(part, part, ws.at[way, i], wr.at[way, i], (z_up, z_down)[way])

    def w_send(i):
        @pl.when(i >= 2)
        def _():
            w_copy_of(i - 2, 0, 1).wait_recv()
            w_copy_of(i - 2, 1, 1).wait_recv()

        w_copy_of(i, 0, 0).start()
        w_copy_of(i, 1, 0).start()

    z_both(z, 0, 1, z_up).start()
    z_both(z, 7, 2, z_down).start()
    x_first(0, 0, x).start()
    x_first(0, 1, x).start()
    w_copy.wait()
    w_send(0)
    w_send(1)

    rows_at = lax.broadcasted_iota(jnp.int32, (SLOTS, HD), 0)

    def mark(c, carry):
        block = (rows_at < lengths[c]).astype(jnp.float32).astype(jnp.bfloat16)
        live[lax.div(c, NX), span(lax.rem(c, NX)), :] = block
        return carry

    lax.fori_loop(0, NZ * NX, mark, 0)

    z_arrival(1)
    z_forward(1, lambda copy: copy.start())
    x_start(1)
    x_forward(0)

    def attend(zp, first):
        def head(h, carry):
            query = q[:, pl.ds(pl.multiple_of(h * HD, HD), HD)]
            s = lax.dot_general(
                query, kv[zp, 0], (((1,), (1,)), ((), ())), preferred_element_type=jnp.float32
            )
            if first:
                slot = x * SLOTS + lax.broadcasted_iota(jnp.int32, (SLOTS, KEYS), 0)
                at = lax.broadcasted_iota(jnp.int32, (SLOTS, KEYS), 1)
                s = jnp.where(at <= slot, s, -1e30)
            top = jnp.max(s, axis=1, keepdims=True)
            if not first:
                before = peak[h][:, 0:1]
                top = jnp.maximum(top, before)
            weights = jnp.exp2(s * SCALE - top * SCALE).astype(jnp.bfloat16)
            terms = jnp.concatenate([kv[zp, 1], live[zp]], axis=1)
            part = jnp.dot(weights, terms, preferred_element_type=jnp.float32)
            if first:
                acc[h] = part
            else:
                acc[h] = acc[h] * jnp.exp2((before - top) * SCALE) + part
            peak[h] = jnp.broadcast_to(top, (SLOTS, HD))
            return carry

        lax.fori_loop(0, HEADS, head, 0)

    def chunk(s, carry):
        @pl.when(s <= 5)
        def _():
            z_arrival(s + 2)
            z_forward(s + 2, lambda copy: copy.start())

        @pl.when(s <= 6)
        def _():
            x_forward(s + 1)

        @pl.when(s <= 5)
        def _():
            x_start(s + 2)

        @pl.when((s >= 2) & (s <= 6))
        def _():
            w_send(s)

        @pl.when(needed(s))
        def _():
            x_second(s, 0, across).wait_recv()
            x_second(s, 1, across).wait_recv()

        @pl.when(s == 0)
        def _():
            attend(z, True)

        @pl.when((s > 0) & needed(s))
        def _():
            attend(zp_of(s), False)

        return carry

    lax.fori_loop(0, NZ, chunk, 0)

    def a_first(r, way):
        block = abuf.at[x, r]
        return remote(block, block, as1.at[way, r], ar.at[2 - way, r], (x_right, x_left)[way])

    def a_second(way):
        block = abuf.at[(left, right)[way], way]
        return remote(block, block, as2.at[way], ar.at[3, way], (x_right, x_left)[way])

    def finish(r, carry):
        rows = pl.ds(pl.multiple_of(r * HALF, HALF), HALF)
        kept = lax.broadcasted_iota(jnp.int32, (HALF, HD), 0) + r * HALF < own_length

        def head(h, inner):
            a = acc[h, rows, :]
            o = jnp.where(kept, a[:, :HD] / a[:, HD:], 0.0).astype(jnp.bfloat16)
            abuf[x, r, :, pl.ds(pl.multiple_of(h * HD, HD), HD)] = o
            return inner

        lax.fori_loop(0, HEADS, head, 0)
        a_first(r, 0).start()
        a_first(r, 1).start()
        return carry

    lax.fori_loop(0, 2, finish, 0)
    for i in (5, 6):
        w_copy_of(i, 0, 1).wait_recv()
        w_copy_of(i, 1, 1).wait_recv()

    def twin_copy(u):
        return remote(csend.at[u], crecv.at[u], cs.at[u], cr.at[u], twin)

    def relay(u, way):
        return remote(
            rsend.at[u, way], rrecv.at[u, way], rs.at[u, way], rr.at[u, way], (y_up, y_down)[way]
        )

    def main(u, way):
        return remote(
            msend.at[u, way], mrecv.at[u, way], ms.at[u, way], mr.at[u, way], (y_up, y_down)[way]
        )

    def home(u, i, r):
        place = obuf.at[
            pl.ds(pl.multiple_of(r * HALF, HALF), HALF), pl.ds(pl.multiple_of(x * WIDE, WIDE), WIDE)
        ]
        seen = 3 - i + 3 * lax.div(i, 3)
        device = (z * NX + ring(x + x_offset(i), NX), me_t)
        return remote(fbuf.at[u], place, fs.at[u], fr.at[seen, r], device)

    def project(u):
        i, r = unit_place(u)
        column = ring(x + x_offset(i), NX)

        @pl.when(i > 0)
        def _():
            block = abuf.at[column, r]
            remote(block, block, as2.at[0], ar.at[i, r], x_right).wait_recv()

        @pl.when(u == 3)
        def _():
            a_second(0).start()

        @pl.when(u == 4)
        def _():
            a_second(1).start()

        def theirs(j, carry):
            csend[u, j] = jnp.dot(
                abuf[column, r], wbuf[j * 2 + 1 - core], preferred_element_type=jnp.float32
            ).astype(jnp.bfloat16)
            return carry

        lax.fori_loop(0, NY, theirs, 0)
        twin_copy(u).start()

        def ours(j, carry):
            own[u, j] = jnp.dot(
                abuf[column, r], wbuf[j * 2 + core], preferred_element_type=jnp.float32
            )
            return carry

        lax.fori_loop(0, NY, ours, 0)

    def both(u, j):
        return own[u, j] + crecv[u, j].astype(jnp.float32)

    def add_twin(u):
        twin_copy(u).wait_recv()
        total = both(u, ring(y + 2, NY)).astype(jnp.bfloat16)
        rsend[u, 0] = total[:, :HD]
        rsend[u, 1] = total[:, HD:]
        relay(u, 0).start()
        relay(u, 1).start()

    def add_relay(u):
        relay(u, 0).wait_recv()
        relay(u, 1).wait_recv()
        total = both(u, ring(y + 1, NY))
        msend[u, 0, :, :HD] = (total[:, :HD] + rrecv[u, 0].astype(jnp.float32)).astype(jnp.bfloat16)
        msend[u, 0, :, HD:] = total[:, HD:].astype(jnp.bfloat16)
        main(u, 0).start()
        total = both(u, ring(y - 1, NY))
        msend[u, 1, :, :HD] = total[:, :HD].astype(jnp.bfloat16)
        msend[u, 1, :, HD:] = (total[:, HD:] + rrecv[u, 1].astype(jnp.float32)).astype(jnp.bfloat16)
        main(u, 1).start()

    def add_main(u):
        main(u, 0).wait_recv()
        main(u, 1).wait_recv()
        total = both(u, y) + mrecv[u, 0].astype(jnp.float32) + mrecv[u, 1].astype(jnp.float32)
        total = total.astype(jnp.bfloat16)
        i, r = unit_place(u)

        @pl.when(i == 0)
        def _():
            obuf[
                pl.ds(pl.multiple_of(r * HALF, HALF), HALF),
                pl.ds(pl.multiple_of(x * WIDE, WIDE), WIDE),
            ] = total

        @pl.when(i > 0)
        def _():
            fbuf[u] = total
            home(u, i, r).start()

    def unit(n, carry):
        @pl.when((n >= 1) & (n <= UNITS))
        def _():
            add_twin(n - 1)

        @pl.when((n >= 2) & (n <= UNITS + 1))
        def _():
            add_relay(n - 2)

        @pl.when(n >= 3)
        def _():
            add_main(n - 3)

        @pl.when(n < UNITS)
        def _():
            project(n)

        return carry

    lax.fori_loop(0, UNITS + 3, unit, 0)

    def arrived(n, carry):
        i, r = 1 + lax.div(n, 2), lax.rem(n, 2)
        place = obuf.at[
            pl.ds(pl.multiple_of(r * HALF, HALF), HALF),
            pl.ds(pl.multiple_of(ring(x + x_offset(i), NX) * WIDE, WIDE), WIDE),
        ]
        remote(fbuf.at[0], place, fs.at[0], fr.at[i, r], x_right).wait_recv()
        return carry

    lax.fori_loop(0, UNITS - 2, arrived, 0)
    out_copy = pltpu.make_async_copy(obuf, out, local.at[0])
    out_copy.start()

    z_both(z, 0, 1, z_up).wait_send()
    z_both(z, 7, 2, z_down).wait_send()

    def sent_chunk(j, carry):
        @pl.when(j > 0)
        def _():
            z_forward(j, lambda copy: copy.wait_send())

        @pl.when(needed(j))
        def _():
            for way in (0, 1):
                x_first(j, way, x).wait_send()
                x_second(j, way, (left, right)[way]).wait_send()

        @pl.when(j <= 6)
        def _():
            w_copy_of(j, 0, 0).wait_send()
            w_copy_of(j, 1, 0).wait_send()

        return carry

    lax.fori_loop(0, NZ, sent_chunk, 0)
    for way in (0, 1):
        a_first(0, way).wait_send()
        a_first(1, way).wait_send()
        a_second(way).wait_send()

    def sent_unit(u, carry):
        twin_copy(u).wait_send()
        for way in (0, 1):
            relay(u, way).wait_send()
            main(u, way).wait_send()

        @pl.when(u >= 2)
        def _():
            i, r = unit_place(u)
            home(u, i, r).wait_send()

        return carry

    lax.fori_loop(0, UNITS, sent_unit, 0)
    out_copy.wait()


def shards(lengths, queries, keys, values, out_weight):
    bf16, f32 = jnp.bfloat16, jnp.float32
    dma = pltpu.SemaphoreType.DMA
    vmem = pl.BlockSpec(memory_space=pltpu.VMEM)
    return pl.pallas_call(
        kernel,
        out_shape=jax.ShapeDtypeStruct(queries.shape, bf16),
        in_specs=[
            pl.BlockSpec(memory_space=pltpu.SMEM), vmem, vmem, vmem, pl.BlockSpec(memory_space=pl.ANY)
        ],
        out_specs=pl.BlockSpec(memory_space=pl.ANY),
        scratch_shapes=[
            pltpu.VMEM((NZ, 2, KEYS, HD), bf16),
            pltpu.VMEM((NZ, KEYS, HD), bf16),
            pltpu.VMEM((HEADS, SLOTS, 2 * HD), f32),
            pltpu.VMEM((HEADS, SLOTS, HD), f32),
            pltpu.VMEM((NZ, DEPTH, WIDE), bf16),
            pltpu.VMEM((NX, 2, HALF, DEPTH), bf16),
            pltpu.VMEM((UNITS, NY, HALF, WIDE), bf16),
            pltpu.VMEM((UNITS, NY, HALF, WIDE), bf16),
            pltpu.VMEM((UNITS, NY, HALF, WIDE), f32),
            pltpu.VMEM((UNITS, 2, HALF, HD), bf16),
            pltpu.VMEM((UNITS, 2, HALF, HD), bf16),
            pltpu.VMEM((UNITS, 2, HALF, WIDE), bf16),
            pltpu.VMEM((UNITS, 2, HALF, WIDE), bf16),
            pltpu.VMEM((UNITS, HALF, WIDE), bf16),
            pltpu.VMEM((SLOTS, DEPTH), bf16),
            dma((1,)),
            dma((8,)), dma((9,)),
            dma((2, 8)), dma((2, 8)), dma((2, 8)), dma((2, 8)),
            dma((2, 7)), dma((2, 7)),
            dma((2, 2)), dma((2,)), dma((4, 2)),
            dma((UNITS,)), dma((UNITS,)),
            dma((UNITS, 2)), dma((UNITS, 2)),
            dma((UNITS, 2)), dma((UNITS, 2)),
            dma((UNITS,)), dma((4, 2)),
        ],
        compiler_params=pltpu.CompilerParams(
            collective_id=0, has_side_effects=True, vmem_limit_bytes=56 * 1024 * 1024
        ),
        cost_estimate=pl.CostEstimate(
            flops=16_000_000_000, bytes_accessed=4_000_000, transcendentals=21_000_000
        ),
    )(lengths, queries, keys, values, out_weight)


def solution(mesh):
    return jax.shard_map(
        shards,
        mesh=mesh,
        in_specs=(P(), P("ctx", "tp"), P("ctx", "tp"), P("ctx", "tp"), P("tp", "ctx")),
        out_specs=P("ctx", "tp"),
        check_vma=False,
    )
```

time: 511 us -> 139 us (0.27)
  the two profiles are of different devices: /device:TPU:1 before, /device:TPU:224 now
where the time goes in v1:
time: 139 us
  Pallas kernels  137 us (99%)
  local copies, waits for them, and re-layouts  1.92 us (1%)
    pallas_call x1, Pallas kernels, shards(): pl.pallas_call(kernel, out_shape=jax.ShapeDtypeStruct(queries.shape, bf16...  137 us

profile of v1, /device:TPU:224, one launch (start us, length us, event | category | flops | bytes accessed | tf_op | source)
XLA Modules:
  0.0 138.9 jit_solution(16067992372553232837)
XLA Ops:
  0.0 137.0 %shard_map.55 = bf16[288,1024]{1,0:T(8,128)(2,1)} custom-call(s32[32]{0:T(128)} %lengths.1, bf16[288,1024]{1,0:T(8,128)(2,1)} %q.1, bf16[288,128]{1,0:T(8,128)(2,1)} %k.1, bf16[288,128]{1,0:T(8,128)(2,1)} %v.1, bf16[1024,256]{1,0:T(8,128)(2,1)} %w.1), custom_call_target="tpu_custom_call" | custom-call | flops 16000000000 | bytes 4000000 | tf_op jit(solution)/shard_map/pallas_call | solution.py:471
  137.0 1.9 %copy.7 = bf16[288,1024]{1,0:T(8,128)(2,1)} copy(bf16[288,1024]{1,0:T(8,128)(2,1)} %shard_map.55) | data formatting | bytes 1179648

commit v2 on v1

--- a/solution.py
+++ b/solution.py
@@ -15,7 +15,9 @@
 HALF = SLOTS // 2
 WIDE = 256
 DEPTH = 1024
-PIECE = DEPTH // 2
+PARTS = 4
+PIECE = DEPTH // PARTS
+SENDS = 7 * PARTS // 2
 UNITS = 2 * NX
 SCALE = math.log2(math.e) * HD**-0.5
 MESH = pl.DeviceIdType.MESH
@@ -43,8 +45,8 @@
 
 
 def kernel(
-    lengths, q, k, v, w, out,
-    kv, live, acc, peak, wbuf, abuf, csend, crecv, own, rsend, rrecv, msend, mrecv, fbuf, obuf,
+    lengths, q_in, k, v, w, out,
+    q, kv, live, acc, peak, wbuf, abuf, csend, crecv, own, rsend, rrecv, msend, mrecv, fbuf, obuf,
     local, zs, zr, xs1, xr1, xs2, xr2, ws, wr, as1, as2, ar, cs, cr, rs, rr, ms, mr, fs, fr,
 ):
     me_c = lax.axis_index("ctx")
@@ -78,6 +80,8 @@
 
     w_copy = pltpu.make_async_copy(w, wbuf.at[z], local.at[0])
     w_copy.start()
+    q_copy = pltpu.make_async_copy(q_in, q, local.at[1])
+    q_copy.start()
 
     def span(column):
         return pl.ds(pl.multiple_of(column * SLOTS, SLOTS), SLOTS)
@@ -163,28 +167,31 @@
             x_second(j, 1, right).start()
 
     def w_copy_of(i, way, held):
-        hop = lax.div(i, 2) + held
-        half = lax.rem(i, 2) if way == 0 else 1 - lax.rem(i, 2)
+        hop = lax.div(i, PARTS) + held
+        turn = lax.rem(i, PARTS)
+        at = turn if way == 0 else PARTS - 1 - turn
         block = ring(z - hop, NZ) if way == 0 else ring(z + hop, NZ)
-        part = wbuf.at[block, pl.ds(pl.multiple_of(half * PIECE, PIECE), PIECE), :]
+        part = wbuf.at[block, pl.ds(pl.multiple_of(at * PIECE, PIECE), PIECE), :]
         return remote(part, part, ws.at[way, i], wr.at[way, i], (z_up, z_down)[way])
 
     def w_send(i):
-        @pl.when(i >= 2)
-        def _():
-            w_copy_of(i - 2, 0, 1).wait_recv()
-            w_copy_of(i - 2, 1, 1).wait_recv()
+        @pl.when(i >= PARTS)
+        def _():
+            w_copy_of(i - PARTS, 0, 1).wait_recv()
+            w_copy_of(i - PARTS, 1, 1).wait_recv()
 
         w_copy_of(i, 0, 0).start()
         w_copy_of(i, 1, 0).start()
 
+    def z_turn(j):
+        z_arrival(j)
+        z_forward(j, lambda copy: copy.start())
+
     z_both(z, 0, 1, z_up).start()
     z_both(z, 7, 2, z_down).start()
-    x_first(0, 0, x).start()
-    x_first(0, 1, x).start()
+    x_start(0)
     w_copy.wait()
     w_send(0)
-    w_send(1)
 
     rows_at = lax.broadcasted_iota(jnp.int32, (SLOTS, HD), 0)
 
@@ -195,21 +202,37 @@
 
     lax.fori_loop(0, NZ * NX, mark, 0)
 
-    z_arrival(1)
-    z_forward(1, lambda copy: copy.start())
+    z_turn(1)
+    z_turn(2)
+    w_send(1)
+    x_forward(0)
     x_start(1)
-    x_forward(0)
+    x_start(2)
+    z_turn(3)
+    z_turn(4)
+    w_send(2)
+    x_forward(1)
+    x_start(3)
+    w_send(3)
+    q_copy.wait()
 
     def attend(zp, first):
-        def head(h, carry):
-            query = q[:, pl.ds(pl.multiple_of(h * HD, HD), HD)]
-            s = lax.dot_general(
-                query, kv[zp, 0], (((1,), (1,)), ((), ())), preferred_element_type=jnp.float32
+        def score(h):
+            return lax.dot_general(
+                q[:, h * HD:(h + 1) * HD], kv[zp, 0], (((1,), (1,)), ((), ())),
+                preferred_element_type=jnp.float32,
             )
+
+        if first:
+            slot = x * SLOTS + lax.broadcasted_iota(jnp.int32, (SLOTS, KEYS), 0)
+            blocked = lax.broadcasted_iota(jnp.int32, (SLOTS, KEYS), 1) > slot
+        ahead = score(0)
+        for h in range(HEADS):
+            s = ahead
+            if h + 1 < HEADS:
+                ahead = score(h + 1)
             if first:
-                slot = x * SLOTS + lax.broadcasted_iota(jnp.int32, (SLOTS, KEYS), 0)
-                at = lax.broadcasted_iota(jnp.int32, (SLOTS, KEYS), 1)
-                s = jnp.where(at <= slot, s, -1e30)
+                s = jnp.where(blocked, -1e30, s)
             top = jnp.max(s, axis=1, keepdims=True)
             if not first:
                 before = peak[h][:, 0:1]
@@ -222,27 +245,33 @@
             else:
                 acc[h] = acc[h] * jnp.exp2((before - top) * SCALE) + part
             peak[h] = jnp.broadcast_to(top, (SLOTS, HD))
-            return carry
-
-        lax.fori_loop(0, HEADS, head, 0)
 
     def chunk(s, carry):
+        @pl.when(s == 1)
+        def _():
+            z_turn(5)
+            z_turn(6)
+
+        @pl.when(s == 3)
+        def _():
+            z_turn(7)
+
         @pl.when(s <= 5)
         def _():
-            z_arrival(s + 2)
-            z_forward(s + 2, lambda copy: copy.start())
-
-        @pl.when(s <= 6)
-        def _():
-            x_forward(s + 1)
-
-        @pl.when(s <= 5)
-        def _():
-            x_start(s + 2)
-
-        @pl.when((s >= 2) & (s <= 6))
-        def _():
-            w_send(s)
+            x_forward(s + 2)
+
+        @pl.when(s <= 3)
+        def _():
+            x_start(s + 4)
+
+        @pl.when(s >= 1)
+        def _():
+            i = lax.div(3 * s + 5, 2)
+            w_send(i)
+
+            @pl.when(lax.rem(s, 2) == 0)
+            def _():
+                w_send(i + 1)
 
         @pl.when(needed(s))
         def _():
@@ -285,7 +314,7 @@
         return carry
 
     lax.fori_loop(0, 2, finish, 0)
-    for i in (5, 6):
+    for i in range(SENDS - PARTS, SENDS):
         w_copy_of(i, 0, 1).wait_recv()
         w_copy_of(i, 1, 1).wait_recv()
 
@@ -327,22 +356,14 @@
         def _():
             a_second(1).start()
 
-        def theirs(j, carry):
+        rows = abuf[column, r]
+        for j in range(NY):
             csend[u, j] = jnp.dot(
-                abuf[column, r], wbuf[j * 2 + 1 - core], preferred_element_type=jnp.float32
+                rows, wbuf[j * 2 + 1 - core], preferred_element_type=jnp.float32
             ).astype(jnp.bfloat16)
-            return carry
-
-        lax.fori_loop(0, NY, theirs, 0)
         twin_copy(u).start()
-
-        def ours(j, carry):
-            own[u, j] = jnp.dot(
-                abuf[column, r], wbuf[j * 2 + core], preferred_element_type=jnp.float32
-            )
-            return carry
-
-        lax.fori_loop(0, NY, ours, 0)
+        for j in range(NY):
+            own[u, j] = jnp.dot(rows, wbuf[j * 2 + core], preferred_element_type=jnp.float32)
 
     def both(u, j):
         return own[u, j] + crecv[u, j].astype(jnp.float32)
@@ -386,26 +407,35 @@
             fbuf[u] = total
             home(u, i, r).start()
 
-    def unit(n, carry):
-        @pl.when((n >= 1) & (n <= UNITS))
-        def _():
-            add_twin(n - 1)
-
-        @pl.when((n >= 2) & (n <= UNITS + 1))
-        def _():
-            add_relay(n - 2)
-
-        @pl.when(n >= 3)
-        def _():
-            add_main(n - 3)
-
-        @pl.when(n < UNITS)
-        def _():
-            project(n)
-
-        return carry
-
-    lax.fori_loop(0, UNITS + 3, unit, 0)
+    def group(g, carry):
+        def project_one(u, inner):
+            project(u)
+            return inner
+
+        def twin_one(u, inner):
+            add_twin(u)
+            return inner
+
+        def relay_one(u, inner):
+            add_relay(u)
+            return inner
+
+        lax.fori_loop(2 * g, 2 * g + 2, project_one, 0)
+        lax.fori_loop(2 * g, 2 * g + 2, twin_one, 0)
+
+        @pl.when(g > 0)
+        def _():
+            lax.fori_loop(2 * g - 2, 2 * g, main_one, 0)
+
+        lax.fori_loop(2 * g, 2 * g + 2, relay_one, 0)
+        return carry
+
+    def main_one(u, carry):
+        add_main(u)
+        return carry
+
+    lax.fori_loop(0, UNITS // 2, group, 0)
+    lax.fori_loop(UNITS - 2, UNITS, main_one, 0)
 
     def arrived(n, carry):
         i, r = 1 + lax.div(n, 2), lax.rem(n, 2)
@@ -434,14 +464,16 @@
                 x_first(j, way, x).wait_send()
                 x_second(j, way, (left, right)[way]).wait_send()
 
-        @pl.when(j <= 6)
-        def _():
-            w_copy_of(j, 0, 0).wait_send()
-            w_copy_of(j, 1, 0).wait_send()
-
         return carry
 
     lax.fori_loop(0, NZ, sent_chunk, 0)
+
+    def sent_piece(i, carry):
+        w_copy_of(i, 0, 0).wait_send()
+        w_copy_of(i, 1, 0).wait_send()
+        return carry
+
+    lax.fori_loop(0, SENDS, sent_piece, 0)
     for way in (0, 1):
         a_first(0, way).wait_send()
         a_first(1, way).wait_send()
@@ -468,14 +500,16 @@
     bf16, f32 = jnp.bfloat16, jnp.float32
     dma = pltpu.SemaphoreType.DMA
     vmem = pl.BlockSpec(memory_space=pltpu.VMEM)
+    any_space = pl.BlockSpec(memory_space=pl.ANY)
     return pl.pallas_call(
         kernel,
         out_shape=jax.ShapeDtypeStruct(queries.shape, bf16),
         in_specs=[
-            pl.BlockSpec(memory_space=pltpu.SMEM), vmem, vmem, vmem, pl.BlockSpec(memory_space=pl.ANY)
+            pl.BlockSpec(memory_space=pltpu.SMEM), any_space, vmem, vmem, any_space
         ],
-        out_specs=pl.BlockSpec(memory_space=pl.ANY),
+        out_specs=any_space,
         scratch_shapes=[
+            pltpu.VMEM((SLOTS, DEPTH), bf16),
             pltpu.VMEM((NZ, 2, KEYS, HD), bf16),
             pltpu.VMEM((NZ, KEYS, HD), bf16),
             pltpu.VMEM((HEADS, SLOTS, 2 * HD), f32),
@@ -491,10 +525,10 @@
             pltpu.VMEM((UNITS, 2, HALF, WIDE), bf16),
             pltpu.VMEM((UNITS, HALF, WIDE), bf16),
             pltpu.VMEM((SLOTS, DEPTH), bf16),
-            dma((1,)),
+            dma((2,)),
             dma((8,)), dma((9,)),
             dma((2, 8)), dma((2, 8)), dma((2, 8)), dma((2, 8)),
-            dma((2, 7)), dma((2, 7)),
+            dma((2, SENDS)), dma((2, SENDS)),
             dma((2, 2)), dma((2,)), dma((4, 2)),
             dma((UNITS,)), dma((UNITS,)),
             dma((UNITS, 2)), dma((UNITS, 2)),

time: 139 us -> 104 us (0.75)
  the two profiles are of different devices: /device:TPU:224 before, /device:TPU:1 now
where the time goes in v2:
time: 104 us
  Pallas kernels  102 us (98%)
  local copies, waits for them, and re-layouts  1.92 us (2%)
    pallas_call x1, Pallas kernels, shards(): pl.pallas_call(kernel, out_shape=jax.ShapeDtypeStruct(queries.shape, bf16...  102 us

profile of v2, /device:TPU:1, one launch (start us, length us, event | category | flops | bytes accessed | tf_op | source)
XLA Modules:
  0.0 103.5 jit_solution(12443708807175846491)
XLA Ops:
  0.0 101.6 %shard_map.55 = bf16[288,1024]{1,0:T(8,128)(2,1)} custom-call(s32[32]{0:T(128)} %lengths.1, bf16[288,1024]{1,0:T(8,128)(2,1)} %q_in.1, bf16[288,128]{1,0:T(8,128)(2,1)} %k.1, bf16[288,128]{1,0:T(8,128)(2,1)} %v.1, bf16[1024,256]{1,0:T(8,128)(2,1)} %w.1), custom_call_target="tpu_custom_call" | custom-call | flops 16000000000 | bytes 4000000 | tf_op jit(solution)/shard_map/pallas_call | solution.py:504
  101.6 1.9 %copy.7 = bf16[288,1024]{1,0:T(8,128)(2,1)} copy(bf16[288,1024]{1,0:T(8,128)(2,1)} %shard_map.55) | data formatting | bytes 1179648

commit v3 on v2

--- a/solution.py
+++ b/solution.py
@@ -47,7 +47,7 @@
 def kernel(
     lengths, q_in, k, v, w, out,
     q, kv, live, acc, peak, wbuf, abuf, csend, crecv, own, rsend, rrecv, msend, mrecv, fbuf, obuf,
-    local, zs, zr, xs1, xr1, xs2, xr2, ws, wr, as1, as2, ar, cs, cr, rs, rr, ms, mr, fs, fr,
+    local, zs, zr, xs1, xr1, xs2, xr2, ws, wr, as1, as2, ar, ar2, cs, cr, rs, rr, ms, mr, fs, fr,
 ):
     me_c = lax.axis_index("ctx")
     me_t = lax.axis_index("tp")
@@ -216,16 +216,18 @@
     w_send(3)
     q_copy.wait()
 
-    def attend(zp, first):
+    def attend(zp, first, start, count):
+        rows = slice(start, start + count)
+
         def score(h):
             return lax.dot_general(
-                q[:, h * HD:(h + 1) * HD], kv[zp, 0], (((1,), (1,)), ((), ())),
+                q[rows, h * HD:(h + 1) * HD], kv[zp, 0], (((1,), (1,)), ((), ())),
                 preferred_element_type=jnp.float32,
             )
 
         if first:
-            slot = x * SLOTS + lax.broadcasted_iota(jnp.int32, (SLOTS, KEYS), 0)
-            blocked = lax.broadcasted_iota(jnp.int32, (SLOTS, KEYS), 1) > slot
+            slot = x * SLOTS + start + lax.broadcasted_iota(jnp.int32, (count, KEYS), 0)
+            blocked = lax.broadcasted_iota(jnp.int32, (count, KEYS), 1) > slot
         ahead = score(0)
         for h in range(HEADS):
             s = ahead
@@ -235,16 +237,16 @@
                 s = jnp.where(blocked, -1e30, s)
             top = jnp.max(s, axis=1, keepdims=True)
             if not first:
-                before = peak[h][:, 0:1]
+                before = peak[h, rows, :][:, 0:1]
                 top = jnp.maximum(top, before)
             weights = jnp.exp2(s * SCALE - top * SCALE).astype(jnp.bfloat16)
             terms = jnp.concatenate([kv[zp, 1], live[zp]], axis=1)
             part = jnp.dot(weights, terms, preferred_element_type=jnp.float32)
             if first:
-                acc[h] = part
+                acc[h, rows, :] = part
             else:
-                acc[h] = acc[h] * jnp.exp2((before - top) * SCALE) + part
-            peak[h] = jnp.broadcast_to(top, (SLOTS, HD))
+                acc[h, rows, :] = acc[h, rows, :] * jnp.exp2((before - top) * SCALE) + part
+            peak[h, rows, :] = jnp.broadcast_to(top, (count, HD))
 
     def chunk(s, carry):
         @pl.when(s == 1)
@@ -255,10 +257,6 @@
         @pl.when(s == 3)
         def _():
             z_turn(7)
-
-        @pl.when(s <= 5)
-        def _():
-            x_forward(s + 2)
 
         @pl.when(s <= 3)
         def _():
@@ -280,11 +278,15 @@
 
         @pl.when(s == 0)
         def _():
-            attend(z, True)
-
-        @pl.when((s > 0) & needed(s))
-        def _():
-            attend(zp_of(s), False)
+            attend(z, True, 0, SLOTS)
+
+        @pl.when((s > 0) & (s < NZ - 1) & needed(s))
+        def _():
+            attend(zp_of(s), False, 0, SLOTS)
+
+        @pl.when(s <= 5)
+        def _():
+            x_forward(s + 2)
 
         return carry
 
@@ -294,26 +296,24 @@
         block = abuf.at[x, r]
         return remote(block, block, as1.at[way, r], ar.at[2 - way, r], (x_right, x_left)[way])
 
-    def a_second(way):
-        block = abuf.at[(left, right)[way], way]
-        return remote(block, block, as2.at[way], ar.at[3, way], (x_right, x_left)[way])
-
-    def finish(r, carry):
-        rows = pl.ds(pl.multiple_of(r * HALF, HALF), HALF)
+    def a_second(r, way):
+        block = abuf.at[(left, right)[way], r, :, way * (DEPTH // 2):(way + 1) * (DEPTH // 2)]
+        return remote(block, block, as2.at[way, r], ar2.at[way, r], (x_right, x_left)[way])
+
+    for r in range(2):
+        @pl.when(needed(NZ - 1))
+        def _():
+            attend(zp_of(NZ - 1), False, r * HALF, HALF)
+
+        rows = slice(r * HALF, (r + 1) * HALF)
         kept = lax.broadcasted_iota(jnp.int32, (HALF, HD), 0) + r * HALF < own_length
-
-        def head(h, inner):
+        for h in range(HEADS):
             a = acc[h, rows, :]
             o = jnp.where(kept, a[:, :HD] / a[:, HD:], 0.0).astype(jnp.bfloat16)
-            abuf[x, r, :, pl.ds(pl.multiple_of(h * HD, HD), HD)] = o
-            return inner
-
-        lax.fori_loop(0, HEADS, head, 0)
+            abuf[x, r, :, h * HD:(h + 1) * HD] = o
         a_first(r, 0).start()
         a_first(r, 1).start()
-        return carry
-
-    lax.fori_loop(0, 2, finish, 0)
+
     for i in range(SENDS - PARTS, SENDS):
         w_copy_of(i, 0, 1).wait_recv()
         w_copy_of(i, 1, 1).wait_recv()
@@ -343,18 +343,24 @@
         i, r = unit_place(u)
         column = ring(x + x_offset(i), NX)
 
-        @pl.when(i > 0)
+        @pl.when((i == 1) | (i == 2))
         def _():
             block = abuf.at[column, r]
-            remote(block, block, as2.at[0], ar.at[i, r], x_right).wait_recv()
-
-        @pl.when(u == 3)
-        def _():
-            a_second(0).start()
-
-        @pl.when(u == 4)
-        def _():
-            a_second(1).start()
+            remote(block, block, as1.at[0, 0], ar.at[i, r], x_right).wait_recv()
+
+        @pl.when(i == 2)
+        def _():
+            a_second(r, 0).start()
+
+        @pl.when(i == 1)
+        def _():
+            a_second(r, 1).start()
+
+        @pl.when(i == 3)
+        def _():
+            for way in (0, 1):
+                block = abuf.at[across, r, :, way * (DEPTH // 2):(way + 1) * (DEPTH // 2)]
+                remote(block, block, as2.at[way, r], ar2.at[way, r], x_right).wait_recv()
 
         rows = abuf[column, r]
         for j in range(NY):
@@ -407,35 +413,53 @@
             fbuf[u] = total
             home(u, i, r).start()
 
-    def group(g, carry):
-        def project_one(u, inner):
-            project(u)
-            return inner
-
-        def twin_one(u, inner):
-            add_twin(u)
-            return inner
-
-        def relay_one(u, inner):
-            add_relay(u)
-            return inner
-
-        lax.fori_loop(2 * g, 2 * g + 2, project_one, 0)
-        lax.fori_loop(2 * g, 2 * g + 2, twin_one, 0)
-
-        @pl.when(g > 0)
-        def _():
-            lax.fori_loop(2 * g - 2, 2 * g, main_one, 0)
-
-        lax.fori_loop(2 * g, 2 * g + 2, relay_one, 0)
+    def sent_before():
+        z_both(z, 0, 1, z_up).wait_send()
+        z_both(z, 7, 2, z_down).wait_send()
+
+        def sent_chunk(j, carry):
+            @pl.when(j > 0)
+            def _():
+                z_forward(j, lambda copy: copy.wait_send())
+
+            @pl.when(needed(j))
+            def _():
+                for way in (0, 1):
+                    x_first(j, way, x).wait_send()
+                    x_second(j, way, (left, right)[way]).wait_send()
+
+            return carry
+
+        lax.fori_loop(0, NZ, sent_chunk, 0)
+
+        def sent_piece(i, carry):
+            w_copy_of(i, 0, 0).wait_send()
+            w_copy_of(i, 1, 0).wait_send()
+            return carry
+
+        lax.fori_loop(0, SENDS, sent_piece, 0)
+
+    def unit(n, carry):
+        @pl.when(n == 2)
+        def _():
+            sent_before()
+
+        @pl.when((n >= 2) & (n < UNITS + 2))
+        def _():
+            add_relay(n - 2)
+
+        @pl.when(n >= 4)
+        def _():
+            add_main(n - 4)
+
+        @pl.when(n < UNITS)
+        def _():
+            project(n)
+            add_twin(n)
+
         return carry
 
-    def main_one(u, carry):
-        add_main(u)
-        return carry
-
-    lax.fori_loop(0, UNITS // 2, group, 0)
-    lax.fori_loop(UNITS - 2, UNITS, main_one, 0)
+    lax.fori_loop(0, UNITS + 4, unit, 0)
 
     def arrived(n, carry):
         i, r = 1 + lax.div(n, 2), lax.rem(n, 2)
@@ -450,34 +474,11 @@
     out_copy = pltpu.make_async_copy(obuf, out, local.at[0])
     out_copy.start()
 
-    z_both(z, 0, 1, z_up).wait_send()
-    z_both(z, 7, 2, z_down).wait_send()
-
-    def sent_chunk(j, carry):
-        @pl.when(j > 0)
-        def _():
-            z_forward(j, lambda copy: copy.wait_send())
-
-        @pl.when(needed(j))
-        def _():
-            for way in (0, 1):
-                x_first(j, way, x).wait_send()
-                x_second(j, way, (left, right)[way]).wait_send()
-
-        return carry
-
-    lax.fori_loop(0, NZ, sent_chunk, 0)
-
-    def sent_piece(i, carry):
-        w_copy_of(i, 0, 0).wait_send()
-        w_copy_of(i, 1, 0).wait_send()
-        return carry
-
-    lax.fori_loop(0, SENDS, sent_piece, 0)
     for way in (0, 1):
         a_first(0, way).wait_send()
         a_first(1, way).wait_send()
-        a_second(way).wait_send()
+        a_second(0, way).wait_send()
+        a_second(1, way).wait_send()
 
     def sent_unit(u, carry):
         twin_copy(u).wait_send()
@@ -529,7 +530,7 @@
             dma((8,)), dma((9,)),
             dma((2, 8)), dma((2, 8)), dma((2, 8)), dma((2, 8)),
             dma((2, SENDS)), dma((2, SENDS)),
-            dma((2, 2)), dma((2,)), dma((4, 2)),
+            dma((2, 2)), dma((2, 2)), dma((4, 2)), dma((2, 2)),
             dma((UNITS,)), dma((UNITS,)),
             dma((UNITS, 2)), dma((UNITS, 2)),
             dma((UNITS, 2)), dma((UNITS, 2)),

time: 104 us -> 98.4 us (0.946)
  Pallas kernels: 102 us -> 96.3 us
    pallas_call x1, Pallas kernels: 102 us -> 96.3 us  [shards(): pl.pallas_call(kernel, out_shape=jax.ShapeDtypeStruct(queries.shape, bf16...]
where the time goes in v3:
time: 98.4 us; the launch traced here: 98.2 us
  Pallas kernels  96.3 us (98%)
  local copies, waits for them, and re-layouts  1.92 us (2%)
    pallas_call x1, Pallas kernels, shards(): pl.pallas_call(kernel, out_shape=jax.ShapeDtypeStruct(queries.shape, bf16...  96.3 us

profile of v3, /device:TPU:1, one launch (start us, length us, event | category | flops | bytes accessed | tf_op | source)
XLA Modules:
  0.0 98.2 jit_solution(8102885768332288266)
XLA Ops:
  0.0 96.3 %shard_map.55 = bf16[288,1024]{1,0:T(8,128)(2,1)} custom-call(s32[32]{0:T(128)} %lengths.1, bf16[288,1024]{1,0:T(8,128)(2,1)} %q_in.1, bf16[288,128]{1,0:T(8,128)(2,1)} %k.1, bf16[288,128]{1,0:T(8,128)(2,1)} %v.1, bf16[1024,256]{1,0:T(8,128)(2,1)} %w.1), custom_call_target="tpu_custom_call" | custom-call | flops 16000000000 | bytes 4000000 | tf_op jit(solution)/shard_map/pallas_call | solution.py:505
  96.3 1.9 %copy.7 = bf16[288,1024]{1,0:T(8,128)(2,1)} copy(bf16[288,1024]{1,0:T(8,128)(2,1)} %shard_map.55) | data formatting | bytes 1179648

commit v4 on v3

--- a/solution.py
+++ b/solution.py
@@ -271,7 +271,7 @@
             def _():
                 w_send(i + 1)
 
-        @pl.when(needed(s))
+        @pl.when((s < NZ - 2) & needed(s))
         def _():
             x_second(s, 0, across).wait_recv()
             x_second(s, 1, across).wait_recv()
@@ -280,7 +280,7 @@
         def _():
             attend(z, True, 0, SLOTS)
 
-        @pl.when((s > 0) & (s < NZ - 1) & needed(s))
+        @pl.when((s > 0) & (s < NZ - 2) & needed(s))
         def _():
             attend(zp_of(s), False, 0, SLOTS)
 
@@ -301,10 +301,17 @@
         return remote(block, block, as2.at[way, r], ar2.at[way, r], (x_right, x_left)[way])
 
     for r in range(2):
-        @pl.when(needed(NZ - 1))
-        def _():
-            attend(zp_of(NZ - 1), False, r * HALF, HALF)
-
+        def last(s, carry):
+            @pl.when(needed(s))
+            def _():
+                if r == 0:
+                    x_second(s, 0, across).wait_recv()
+                    x_second(s, 1, across).wait_recv()
+                attend(zp_of(s), False, r * HALF, HALF)
+
+            return carry
+
+        lax.fori_loop(NZ - 2, NZ, last, 0)
         rows = slice(r * HALF, (r + 1) * HALF)
         kept = lax.broadcasted_iota(jnp.int32, (HALF, HD), 0) + r * HALF < own_length
         for h in range(HEADS):
@@ -444,22 +451,30 @@
         def _():
             sent_before()
 
-        @pl.when((n >= 2) & (n < UNITS + 2))
-        def _():
-            add_relay(n - 2)
-
-        @pl.when(n >= 4)
-        def _():
-            add_main(n - 4)
+        @pl.when((n >= 3) & (n < UNITS + 3))
+        def _():
+            add_relay(n - 3)
+
+        @pl.when(n >= 6)
+        def _():
+            add_main(n - 6)
 
         @pl.when(n < UNITS)
         def _():
             project(n)
+
+        @pl.when((n < UNITS - 2) & (lax.rem(n, 2) == 1))
+        def _():
+            add_twin(n - 1)
             add_twin(n)
 
+        @pl.when((n >= UNITS - 2) & (n < UNITS))
+        def _():
+            add_twin(n)
+
         return carry
 
-    lax.fori_loop(0, UNITS + 4, unit, 0)
+    lax.fori_loop(0, UNITS + 6, unit, 0)
 
     def arrived(n, carry):
         i, r = 1 + lax.div(n, 2), lax.rem(n, 2)

time: 98.4 us -> 97.1 us (0.987)
  Pallas kernels: 96.3 us -> 95 us
    pallas_call x1, Pallas kernels: 96.3 us -> 95 us  [shards(): pl.pallas_call(kernel, out_shape=jax.ShapeDtypeStruct(queries.shape, bf16...]
where the time goes in v4:
time: 97.1 us; the launch traced here: 96.9 us
  Pallas kernels  95 us (98%)
  local copies, waits for them, and re-layouts  1.92 us (2%)
    pallas_call x1, Pallas kernels, shards(): pl.pallas_call(kernel, out_shape=jax.ShapeDtypeStruct(queries.shape, bf16...  95 us

profile of v4, /device:TPU:1, one launch (start us, length us, event | category | flops | bytes accessed | tf_op | source)
XLA Modules:
  0.0 96.9 jit_solution(8052538685963876300)
XLA Ops:
  0.0 95.0 %shard_map.55 = bf16[288,1024]{1,0:T(8,128)(2,1)} custom-call(s32[32]{0:T(128)} %lengths.1, bf16[288,1024]{1,0:T(8,128)(2,1)} %q_in.1, bf16[288,128]{1,0:T(8,128)(2,1)} %k.1, bf16[288,128]{1,0:T(8,128)(2,1)} %v.1, bf16[1024,256]{1,0:T(8,128)(2,1)} %w.1), custom_call_target="tpu_custom_call" | custom-call | flops 16000000000 | bytes 4000000 | tf_op jit(solution)/shard_map/pallas_call | solution.py:520
  95.0 1.9 %copy.7 = bf16[288,1024]{1,0:T(8,128)(2,1)} copy(bf16[288,1024]{1,0:T(8,128)(2,1)} %shard_map.55) | data formatting | bytes 1179648

commit v5 on v4

--- a/solution.py
+++ b/solution.py
@@ -321,6 +321,19 @@
         a_first(r, 0).start()
         a_first(r, 1).start()
 
+    early = z < NZ - 2
+
+    def a_pass(r, way):
+        block = abuf.at[(left, right)[way], r]
+        remote(block, block, as1.at[way, r], ar.at[2 - way, r], x_right).wait_recv()
+        a_second(r, way).start()
+
+    @pl.when(early)
+    def _():
+        for r in range(2):
+            a_pass(r, 0)
+            a_pass(r, 1)
+
     for i in range(SENDS - PARTS, SENDS):
         w_copy_of(i, 0, 1).wait_recv()
         w_copy_of(i, 1, 1).wait_recv()
@@ -350,18 +363,13 @@
         i, r = unit_place(u)
         column = ring(x + x_offset(i), NX)
 
-        @pl.when((i == 1) | (i == 2))
-        def _():
-            block = abuf.at[column, r]
-            remote(block, block, as1.at[0, 0], ar.at[i, r], x_right).wait_recv()
-
-        @pl.when(i == 2)
-        def _():
-            a_second(r, 0).start()
-
-        @pl.when(i == 1)
-        def _():
-            a_second(r, 1).start()
+        @pl.when((i == 2) & (z >= NZ - 2))
+        def _():
+            a_pass(r, 0)
+
+        @pl.when((i == 1) & (z >= NZ - 2))
+        def _():
+            a_pass(r, 1)
 
         @pl.when(i == 3)
         def _():

time: 97.1 us -> 102 us (1.050)
  Pallas kernels: 95 us -> 99.6 us
    pallas_call x1, Pallas kernels: 95 us -> 99.6 us  [shards(): pl.pallas_call(kernel, out_shape=jax.ShapeDtypeStruct(queries.shape, bf16...]
where the time goes in v5:
time: 102 us; the launch traced here: 101 us
  Pallas kernels  99.6 us (98%)
  local copies, waits for them, and re-layouts  1.92 us (2%)
    pallas_call x1, Pallas kernels, shards(): pl.pallas_call(kernel, out_shape=jax.ShapeDtypeStruct(queries.shape, bf16...  99.6 us

profile of v5, /device:TPU:1, one launch (start us, length us, event | category | flops | bytes accessed | tf_op | source)
XLA Modules:
  0.0 101.5 jit_solution(11894500545565901605)
XLA Ops:
  0.0 99.6 %shard_map.55 = bf16[288,1024]{1,0:T(8,128)(2,1)} custom-call(s32[32]{0:T(128)} %lengths.1, bf16[288,1024]{1,0:T(8,128)(2,1)} %q_in.1, bf16[288,128]{1,0:T(8,128)(2,1)} %k.1, bf16[288,128]{1,0:T(8,128)(2,1)} %v.1, bf16[1024,256]{1,0:T(8,128)(2,1)} %w.1), custom_call_target="tpu_custom_call" | custom-call | flops 16000000000 | bytes 4000000 | tf_op jit(solution)/shard_map/pallas_call | solution.py:528
  99.6 1.9 %copy.7 = bf16[288,1024]{1,0:T(8,128)(2,1)} copy(bf16[288,1024]{1,0:T(8,128)(2,1)} %shard_map.55) | data formatting | bytes 1179648
